TPU v7x, 32 devices: a whole 2x2x4 slice. The times are simulated.
32 devices in a mesh: grp: 2 (over y), node: 4 (over x, core), chip: 4 (over z).
Axes of the slice: x: 2, y: 2, z: 4, core: 2. Of those that a mesh axis runs over, the one named last changes fastest.
Arguments:
- tokens: bfloat16 [4096, 7168], P(('grp', 'node', 'chip')), parts along dimension 0, may hold values from -31 to 31
- norm_gain: float32 [7168], replicated, may hold values from 0.1 to 1.9
- expert_ids: int32 [4096, 8], P(('grp', 'node', 'chip')), parts along dimension 0, may hold values from 0 to 383, as said below
- gate_num: int32 [4096, 8], P(('grp', 'node', 'chip')), parts along dimension 0, may hold values from 1 to 4096
- node_mask: int32 [4096, 4], P(('grp', 'node', 'chip')), parts along dimension 0, may hold values from 0 to 1, as said below
- w_gate: bfloat16 [4, 7168, 1024], P('node', 'chip'), may hold values from -0.0625 to 0.0625
- w_up: bfloat16 [4, 7168, 1024], P('node', 'chip'), may hold values from -0.0625 to 0.0625
- w_down: bfloat16 [4, 1024, 7168], P('node', None, 'chip'), may hold values from -0.1875 to 0.1875
Outputs:
- mixed: bfloat16 [4096, 7168], P(('grp', 'node', 'chip')), parts along dimension 0
There are 2 independent parts, one for each index of `grp`. A program takes and returns all parts, laid end to end along the dimension named above; an argument that names none is the same for every part. Nothing has to cross between parts.
Inputs may be any that keep to these rules, and one draw needn't show every extreme that they name: `expert_ids`: each row names 8 different experts; expert e lives on node e // 96, and a row's experts lie on at most 4 nodes. Exactly one id of each row is a multiple of 96. Among the 128 rows of one device no such id is named more than 64 times. `node_mask`: each row has at most 4 ones, all at nodes of the row's experts.
All inputs are finite; a program needn't handle non-finite values.
Results may differ from a plain program's by a relative error of at most 0.0038.
Values may be sent and summed in bfloat16 or wider, within the bound.
A program may use at most 128 MiB of HBM per device.

v0:
```python
import jax
import jax.numpy as jnp
from jax import lax
from jax.sharding import PartitionSpec as P

EXPERTS = 384
DEN = 4096


ROUTE_SCALE = 2.827


def body(tokens, norm_gain, expert_ids, gate_num, node_mask, w_gate, w_up, w_down):
    node_count = lax.axis_size("node")
    chip_count = lax.axis_size("chip")
    rows_here, width = tokens.shape
    slice_width = width // chip_count
    hidden_units = w_gate.shape[2]
    exp_node = EXPERTS // node_count
    capacity = 2 * rows_here // node_count
    stream = tokens.astype(jnp.float32)
    inverse_rms = lax.rsqrt(jnp.mean(stream * stream, axis=1, keepdims=True) + 1e-06)
    normed = (stream * inverse_rms * norm_gain).astype(jnp.bfloat16)
    is_first = expert_ids % exp_node == 0
    target_node = jnp.sum(jnp.where(is_first, expert_ids // exp_node, 0), axis=1)
    numerator = jnp.sum(jnp.where(is_first, gate_num, 0), axis=1)
    allowed = jnp.take_along_axis(node_mask, target_node[:, None], axis=1)[:, 0]
    route_weight = (numerator * allowed).astype(jnp.float32) * (ROUTE_SCALE / DEN)
    node_ids = jnp.arange(node_count, dtype=jnp.int32)
    onehot = ((target_node[:, None] == node_ids[None, :]) & (allowed[:, None] == 1)).astype(
        jnp.int32
    )
    position = jnp.sum((jnp.cumsum(onehot, axis=0) - 1) * onehot, axis=1)
    dest_node = jnp.where(allowed == 1, target_node, node_count)
    pieces = normed.reshape(rows_here, chip_count, slice_width)
    outgoing = jnp.zeros((node_count, chip_count, capacity, slice_width), jnp.bfloat16)
    outgoing = outgoing.at[dest_node, :, position, :].set(pieces, mode="drop")
    arrived = lax.all_to_all(
        outgoing.reshape(node_count * chip_count, capacity, slice_width),
        ("node", "chip"),
        split_axis=0,
        concat_axis=0,
        tiled=True,
    )
    received = arrived.reshape(-1, slice_width)
    w_both = jnp.concatenate([w_gate[0], w_up[0]], axis=1)
    own_terms = lax.psum_scatter(
        jnp.dot(received, w_both, preferred_element_type=jnp.float32),
        "chip",
        scatter_dimension=0,
        tiled=True,
    )
    hidden = (jax.nn.silu(own_terms[:, :hidden_units]) * own_terms[:, hidden_units:]).astype(
        jnp.bfloat16
    )
    produced = jnp.dot(
        lax.all_gather(hidden, "chip", axis=0, tiled=True),
        w_down[0],
        preferred_element_type=jnp.float32,
    ).astype(jnp.bfloat16)
    returned = lax.all_to_all(
        produced.reshape(node_count * chip_count, capacity, slice_width),
        ("node", "chip"),
        split_axis=0,
        concat_axis=0,
        tiled=True,
    )
    returned = returned.reshape(node_count, chip_count, capacity, slice_width)
    picked = returned[target_node, :, position, :].reshape(rows_here, width)
    return (stream + route_weight[:, None] * picked.astype(jnp.float32)).astype(jnp.bfloat16)


def solution(mesh):
    placed = (
        P(("grp", "node", "chip"), None),
        P(),
        P(("grp", "node", "chip"), None),
        P(("grp", "node", "chip"), None),
        P(("grp", "node", "chip"), None),
        P("node", "chip", None),
        P("node", "chip", None),
        P("node", None, "chip"),
    )
    return jax.shard_map(
        body,
        mesh=mesh,
        in_specs=placed,
        out_specs=P(("grp", "node", "chip"), None),
        check_vma=False,
    )
```

profile of v0, /device:TPU:25, one launch (start us, length us, event | category | flops | bytes accessed | tf_op | source)
XLA Modules:
  0.0 445.8 jit_solution(14554110359591315733)
XLA Ops:
  6.5 0.0 copy-start
  6.5 0.0 copy-start.1
  6.5 0.0 reduce-scatter.2.cloned.1.call-start
  6.5 2.1 fusion.4
  8.6 0.7 select_reduce_fusion.1
  9.4 0.0 copy-done
  9.4 1.5 gather_fusion.1
  10.9 0.1 fusion.11
  11.0 0.2 reduce_window_sum.11
  11.2 0.2 select_reduce_fusion
  11.4 0.0 copy-done.1
  11.4 2.5 fusion.6
  13.9 4.5 %reshape.153 = bf16[128,4,1792]{2,1,0:T(4,128)(2,1)} reshape(bf16[128,7168]{1,0:T(8,128)(2,1)} %fusion.6) | data formatting | bytes 3670016 | tf_op jit(solution)/shard_map/reshape | solution.py:35
  18.4 2.7 broadcast_in_dim.14
  21.2 18.8 %scatter_fusion = bf16[4,4,64,1792]{3,1,2,0:T(4,128)(2,1)} fusion(bf16[4,4,64,1792]{3,1,2,0:T(4,128)(2,1)} %broadcast_in_dim.14, s32[128]{0:T(128)S(1)} %get-tuple-element.10, bf16[128,4,1792]{2,1,0:T(4,128)(2,1)} %reshape.153), kind=kCustom, calls=%fused_computation.2 | custom fusion | bytes 5506048 | tf_op jit(solution)/shard_map/scatter | solution.py:37
  40.0 2.6 copy.10
  42.6 0.0 copy-start.2
  42.6 0.0 copy-start.3
  42.6 86.7 %all_to_all.10 = bf16[16,64,1792]{2,1,0:T(8,128)(2,1)S(1)} all-to-all(bf16[16,64,1792]{2,1,0:T(8,128)(2,1)S(1)} %bitcast.44), channel_id=1, replica_groups=mesh['grp'=2,'node'=4,'chip'=4] {'node','chip'}, dimensions={0} | all-to-all | bytes 7340032 | tf_op jit(solution)/shard_map/all_to_all | solution.py:38
  129.3 0.0 copy-done.2
  129.3 0.0 copy-done.3
  129.3 10.0 %fusion = f32[1024,2048]{1,0:T(8,128)} fusion(bf16[1024,1792]{1,0:T(8,128)(2,1)S(1)} %bitcast.48, bf16[1792,1024]{1,0:T(8,128)(2,1)S(1)} %bitcast.50, bf16[1792,1024]{1,0:T(8,128)(2,1)S(1)} %bitcast.51), kind=kOutput, calls=%fused_computation.3 | convolution fusion | flops 7530872832 | bytes 19398656 | tf_op jit(solution)/shard_map/dot_general | solution.py:48
  139.3 0.0 reduce-scatter.2.cloned.1.call-update
  139.3 0.2 all-gather.2.cloned.1.call-start
  139.6 145.0 %reduce-scatter.2.cloned.1.call-done = f32[256,2048]{1,0:T(8,128)} async-done(((f32[1024,2048]{1,0:T(8,128)}), f32[256,2048]{1,0:T(8,128)}) %reduce-scatter.2.cloned.1.call-update) | async-done | bytes 2097168 | tf_op jit(solution)/shard_map/reduce_scatter | solution.py:47
  284.6 2.6 fusion.9
  287.2 0.0 all-gather.2.cloned.1.call-update
  287.2 45.2 %all-gather.2.cloned.1.call-done = bf16[1024,1024]{1,0:T(8,128)(2,1)} async-done(((bf16[256,1024]{1,0:T(8,128)(2,1)}), bf16[1024,1024]{1,0:T(8,128)(2,1)}) %all-gather.2.cloned.1.call-update) | async-done | bytes 2097168 | tf_op jit(solution)/shard_map/all_gather | solution.py:57
  332.4 6.6 %convolution_convert_fusion = bf16[1024,1792]{1,0:T(8,128)(2,1)S(1)} fusion(bf16[1024,1024]{1,0:T(8,128)(2,1)} %all-gather.2.cloned.1.call-done, bf16[1,1024,1792]{2,1,0:T(8,128)(2,1)} %param.15), kind=kOutput, calls=%fused_computation.10 | convolution fusion | flops 3759931392 | bytes 9437184 | tf_op jit(solution)/shard_map/dot_general | solution.py:56
  339.0 86.2 %all_to_all.11 = bf16[16,64,1792]{2,1,0:T(8,128)(2,1)S(1)} all-to-all(bf16[16,64,1792]{2,1,0:T(8,128)(2,1)S(1)} %bitcast.49), channel_id=1, replica_groups=mesh['grp'=2,'node'=4,'chip'=4] {'node','chip'}, dimensions={0} | all-to-all | bytes 7340032 | tf_op jit(solution)/shard_map/all_to_all | solution.py:61
  425.2 4.6 %copy.11 = bf16[4,4,64,1792]{3,1,2,0:T(4,128)(2,1)} copy(bf16[4,4,64,1792]{3,2,1,0:T(8,128)(2,1)S(1)} %bitcast.45) | data formatting | bytes 7340032 | tf_op jit(solution)/shard_map/reshape | solution.py:68
  429.8 5.4 %gather_fusion = bf16[128,4,1792]{2,1,0:T(4,128)(2,1)} fusion(bf16[4,4,64,1792]{3,1,2,0:T(4,128)(2,1)} %copy.11, s32[128]{0:T(128)S(1)} %get-tuple-element.9), kind=kCustom, calls=%fused_computation | custom fusion | bytes 3671040 | tf_op jit(solution)/shard_map/gather | solution.py:69
  435.2 1.9 copy.12
  437.2 1.8 fusion.7
  (8 shorter events, 0.1 us)
Async XLA Ops:
  6.5 2.9 copy-start
  6.5 4.9 %copy-start.1 = (bf16[128,7168]{1,0:T(8,128)(2,1)S(1)}, bf16[128,7168]{1,0:T(8,128)(2,1)}, u32[]{:S(2)}) copy-start(bf16[128,7168]{1,0:T(8,128)(2,1)} %param.8) | copy-start | bytes 5505028
  6.5 278.0 %reduce-scatter.2.cloned.1.call-start = ((), (), s32[]{:S(2)}) async-start(), calls=%async_computation.3 | async-start | bytes 10485760 | tf_op jit(solution)/shard_map/reduce_scatter | solution.py:47
  42.6 86.7 %copy-start.2 = (bf16[1,1792,1024]{2,1,0:T(8,128)(2,1)S(1)}, bf16[1,1792,1024]{2,1,0:T(8,128)(2,1)}, u32[]{:S(2)}) copy-start(bf16[1,1792,1024]{2,1,0:T(8,128)(2,1)} %param.14) | copy-start | bytes 11010052
  42.6 86.7 %copy-start.3 = (bf16[1,1792,1024]{2,1,0:T(8,128)(2,1)S(1)}, bf16[1,1792,1024]{2,1,0:T(8,128)(2,1)}, u32[]{:S(2)}) copy-start(bf16[1,1792,1024]{2,1,0:T(8,128)(2,1)} %param.13) | copy-start | bytes 11010052
  139.3 193.1 %all-gather.2.cloned.1.call-start = ((), (), s32[]{:S(2)}) async-start(), calls=%async_computation.4 | async-start | bytes 2621440 | tf_op jit(solution)/shard_map/all_gather | solution.py:57
Sparse Core Ops, SparseCore 0:
  139.5 145.0 reduce-scatter.1
  287.4 44.9 all-gather.1
where the time goes:
time: 450 us; the launch traced here: 446 us
  waiting for transfers between devices  190 us (42%)
  blocking collectives  173 us (38%)
  local copies, waits for them, and re-layouts  42.1 us (9%)
  matrix products  16.6 us (4%)
  between operations  13.5 us (3%)
  other arithmetic  10.2 us (2%)
    reduce_scatter x1, waiting for transfers between devices, body(): lax.psum_scatter(jnp.dot(received, w_both, preferred_element_type=jnp.flo...  145 us
    all_to_all x1, blocking collectives, body(): lax.all_to_all(outgoing.reshape(node_count * chip_count, capacity, slice_...  86.7 us
    all_to_all x1, blocking collectives, body(): lax.all_to_all(produced.reshape(node_count * chip_count, capacity, slice_...  86.2 us
    all_gather x1, waiting for transfers between devices, body(): lax.all_gather(hidden, 'chip', axis=0, tiled=True)  45.2 us
    scatter x2, local copies, waits for them, and re-layouts, body(): outgoing = outgoing.at[dest_node, :, position, :].set(pieces, mode='drop')  21.4 us
    dot_general x1, matrix products, body(): jnp.dot(received, w_both, preferred_element_type=jnp.float32)  10 us
  transfers between devices with their start and end apart: 2, of which 2 were waited for; matrix products, arithmetic and copies ran while one was open for 0% of the time, Pallas kernels for 0%

commit v1 on v0

v1 whole, which is shorter than its diff:
```python
import functools

import jax
import jax.numpy as jnp
from jax import lax
from jax.experimental import pallas as pl
from jax.experimental.pallas import tpu as pltpu
from jax.sharding import PartitionSpec as P

EXPERTS = 384
DEN = 4096
ROUTE_SCALE = 2.827
F32 = jnp.float32
BF16 = jnp.bfloat16


def kernel(
    N, C, cap,
    tok, gain, slot_in, weight, wg_hbm, wu_hbm, wd_hbm,
    out,
    normed, held, slots, packed, rows, wgu, wd, partial, sums, hidden, made, back, final,
    w_sem, ss_sem, sr_sem, as_sem, ar_sem, bs_sem, br_sem, cs_sem, cr_sem,
    hs_sem, hr_sem, ds_sem, dr_sem, es_sem, er_sem,
):
    n = lax.axis_index("node")
    c = lax.axis_index("chip")
    T, D = tok.shape
    SW = D // C
    FF = wd.shape[0]
    B = N * cap
    R = B // 4
    K = 2 * C
    GS = partial.shape[0]
    tile = 256 if SW % 256 == 0 else 128

    def loads():
        return (
            pltpu.make_async_copy(wg_hbm.at[0], wgu.at[:, pl.ds(0, FF)], w_sem.at[0]),
            pltpu.make_async_copy(wu_hbm.at[0], wgu.at[:, pl.ds(FF, FF)], w_sem.at[1]),
            pltpu.make_async_copy(wd_hbm.at[0], wd, w_sem.at[2]),
        )

    for copy in loads():
        copy.start()

    barrier = pltpu.get_barrier_semaphore()

    @pl.loop(1, C)
    def _(r):
        pl.semaphore_signal(barrier, inc=1, device_id={"chip": lax.rem(c + r, C)}, device_id_type=pl.DeviceIdType.MESH)

    @pl.loop(1, N)
    def _(r):
        pl.semaphore_signal(barrier, inc=1, device_id={"node": lax.rem(n + r, N)}, device_id_type=pl.DeviceIdType.MESH)

    def remote(src, dst, ssem, rsem, **device):
        return pltpu.make_async_remote_copy(
            src_ref=src, dst_ref=dst, send_sem=ssem, recv_sem=rsem,
            device_id=device, device_id_type=pl.DeviceIdType.MESH,
        )

    def slot_copy(to, src):
        return remote(slot_in, slots.at[src], ss_sem.at[to], sr_sem.at[src], chip=to)

    def a_copy(to, src):
        return remote(normed.at[to], held.at[src], as_sem.at[to], ar_sem.at[src], chip=to)

    def b_copy(b, to, src):
        return remote(
            packed.at[b, pl.ds(pl.multiple_of(to * cap, cap), cap)],
            rows.at[b, pl.ds(pl.multiple_of(src * cap, cap), cap)],
            bs_sem.at[b, to], br_sem.at[b, src], node=to)

    def c_copy(d, k, to):
        return remote(sums.at[d, k], sums.at[d, k], cs_sem.at[d, k], cr_sem.at[d, k], chip=to)

    def place(d, k):
        return lax.div(k, 2), pl.multiple_of(d * 2 * R + lax.rem(k, 2) * R, R)

    def h_copy(d, k, to):
        b, r = place(d, k)
        piece = hidden.at[b, pl.ds(r, R)]
        return remote(piece, piece, hs_sem.at[d, k], hr_sem.at[d, k], chip=to)

    def d_copy(b, to, src):
        return remote(
            made.at[b, pl.ds(pl.multiple_of(to * cap, cap), cap)],
            back.at[b, pl.ds(pl.multiple_of(src * cap, cap), cap)],
            ds_sem.at[b, to], dr_sem.at[b, src], node=to)

    def e_copy(to, src):
        return remote(held.at[to], final.at[src], es_sem.at[to], er_sem.at[src], chip=to)

    def squares(i, acc):
        v = tok[:, pl.ds(pl.multiple_of(i * tile, tile), tile)].astype(F32)
        return acc + v * v

    acc = lax.fori_loop(0, D // tile, squares, jnp.zeros((T, tile), F32))
    inverse = lax.rsqrt(jnp.sum(acc, axis=1, keepdims=True) * (1.0 / D) + 1e-06)

    pl.semaphore_wait(barrier, C + N - 2)

    def normalise(to):
        @pl.loop(0, SW // tile)
        def _(i):
            col = pl.multiple_of(to * SW + i * tile, tile)
            v = tok[:, pl.ds(col, tile)].astype(F32)
            v = v * inverse * gain[:, pl.ds(col, tile)]
            normed[to, :, pl.ds(pl.multiple_of(i * tile, tile), tile)] = v.astype(BF16)

    @pl.loop(1, C)
    def _(r):
        to = lax.rem(c + r, C)
        slot_copy(to, c).start()
        normalise(to)
        a_copy(to, c).start()

    normalise(c)

    def route(source, b, rows_of_slots):
        @pl.loop(0, SW // tile)
        def _(i):
            col = pl.ds(pl.multiple_of(i * tile, tile), tile)
            packed[b, :, col] = jnp.dot(
                rows_of_slots, source[b, :, col], preferred_element_type=F32).astype(BF16)

        @pl.loop(1, N)
        def _(r):
            b_copy(b, lax.rem(n + r, N), n).start()

        own = pl.ds(pl.multiple_of(n * cap, cap), cap)
        rows[b, own, :] = packed[b, own, :]

    def selector(slot_row):
        ids = lax.broadcasted_iota(jnp.int32, (B, T), 0)
        return jnp.where(ids == slot_row, 1.0, 0.0).astype(BF16)

    slots[c] = slot_in[...]
    route(normed, c, selector(slot_in[0:1, :]))

    @pl.loop(1, C)
    def _(r):
        b = lax.rem(c + r, C)
        slot_copy(b, b).wait_recv()
        a_copy(b, b).wait_recv()
        route(held, b, selector(slots[b, 0:1, :]))

    copies = loads()
    copies[0].wait()
    copies[1].wait()
    copies[2].wait()

    ahead = (C - 1) + jnp.maximum(c, C - 1 - c)
    wide = 512
    thin = 16

    @pl.loop(0, K + 2 * (C - 1) + 2)
    def _(t):
        blk = lax.div(t, 2)

        @pl.when((lax.rem(t, 2) == 0) & (blk < C))
        def _():
            @pl.loop(1, N)
            def _(r):
                src = lax.rem(n + r, N)
                b_copy(blk, src, src).wait_recv()

            @pl.loop(0, 2 * FF // wide)
            def _(i):
                col = pl.ds(pl.multiple_of(i * wide, wide), wide)
                partial[lax.rem(blk, GS), :, col] = jnp.dot(
                    rows[blk], wgu[:, col], preferred_element_type=F32)

        for d in (0, 1):
            pos = c if d == 0 else C - 1 - c
            nxt = c + 1 if d == 0 else c - 1
            prv = c - 1 if d == 0 else c + 1
            k = t - pos

            @pl.when((k >= 0) & (k < K) & (pos == 0))
            def _():
                b, r = place(d, k)

                @pl.loop(0, R // thin)
                def _(i):
                    o = pl.multiple_of(i * thin, thin)
                    sums[d, k, pl.ds(o, thin), :] = partial[
                        lax.rem(b, GS), pl.ds(r + o, thin), :].astype(BF16)

                c_copy(d, k, nxt).start()

            @pl.when((k >= 0) & (k < K) & (pos > 0) & (pos < C - 1))
            def _():
                b, r = place(d, k)
                c_copy(d, k, prv).wait_recv()

                @pl.loop(0, R // thin)
                def _(i):
                    o = pl.multiple_of(i * thin, thin)
                    s = sums[d, k, pl.ds(o, thin), :].astype(F32)
                    s += partial[lax.rem(b, GS), pl.ds(r + o, thin), :]
                    sums[d, k, pl.ds(o, thin), :] = s.astype(BF16)

                c_copy(d, k, nxt).start()

            @pl.when((k >= 0) & (k < K) & (pos == C - 1))
            def _():
                b, r = place(d, k)
                c_copy(d, k, prv).wait_recv()

                @pl.loop(0, R // thin)
                def _(i):
                    o = pl.multiple_of(i * thin, thin)
                    s = sums[d, k, pl.ds(o, thin), :].astype(F32)
                    s += partial[lax.rem(b, GS), pl.ds(r + o, thin), :]
                    g, u = s[:, :FF], s[:, FF:]
                    hidden[b, pl.ds(r + o, thin), :] = (
                        g * (1.0 / (1.0 + jnp.exp(-g))) * u).astype(BF16)

                h_copy(d, k, prv).start()

        for d in (0, 1):
            pos = c if d == 0 else C - 1 - c
            nxt = c + 1 if d == 0 else c - 1
            prv = c - 1 if d == 0 else c + 1
            k = t - 2 * (C - 1) + pos

            @pl.when((k >= 0) & (k < K) & (pos < C - 1))
            def _():
                h_copy(d, k, nxt).wait_recv()

                @pl.when(pos > 0)
                def _():
                    h_copy(d, k, prv).start()

        e = t - ahead

        @pl.when((e >= 0) & (lax.rem(e, 2) == 1) & (e < K))
        def _():
            b = lax.div(e, 2)

            @pl.loop(0, SW // tile)
            def _(i):
                col = pl.ds(pl.multiple_of(i * tile, tile), tile)
                made[b, :, col] = jnp.dot(
                    hidden[b], wd[:, col], preferred_element_type=F32).astype(BF16)

            @pl.loop(1, N)
            def _(r):
                d_copy(b, lax.rem(n + r, N), n).start()

            own = pl.ds(pl.multiple_of(n * cap, cap), cap)
            back[b, own, :] = made[b, own, :]

        f = t - ahead - 2

        @pl.when((f >= 0) & (lax.rem(f, 2) == 1) & (f < K))
        def _():
            b = lax.div(f, 2)

            @pl.loop(1, N)
            def _(r):
                src = lax.rem(n + r, N)
                d_copy(b, src, src).wait_recv()

            pick = selector(slots[b, 0:1, :])

            def give(place_to):
                @pl.loop(0, SW // tile)
                def _(i):
                    col = pl.ds(pl.multiple_of(i * tile, tile), tile)
                    place_to[b, :, col] = lax.dot_general(
                        pick, back[b, :, col], (((0,), (0,)), ((), ())),
                        preferred_element_type=F32).astype(BF16)

            @pl.when(b == c)
            def _():
                give(final)

            @pl.when(b != c)
            def _():
                give(held)
                e_copy(b, c).start()

    def finish(src):
        @pl.loop(0, SW // tile)
        def _(i):
            col = pl.ds(pl.multiple_of(src * SW + i * tile, tile), tile)
            v = final[src, :, pl.ds(pl.multiple_of(i * tile, tile), tile)].astype(F32)
            out[:, col] = (tok[:, col].astype(F32) + weight[...] * v).astype(BF16)

    finish(c)

    @pl.loop(1, C)
    def _(r):
        src = lax.rem(c + r, C)
        e_copy(src, src).wait_recv()
        finish(src)

    @pl.loop(1, C)
    def _(r):
        to = lax.rem(c + r, C)
        slot_copy(to, c).wait_send()
        a_copy(to, c).wait_send()
        e_copy(to, c).wait_send()

    @pl.loop(0, C)
    def _(b):
        @pl.loop(1, N)
        def _(r):
            to = lax.rem(n + r, N)
            b_copy(b, to, n).wait_send()
            d_copy(b, to, n).wait_send()

    for d in (0, 1):
        pos = c if d == 0 else C - 1 - c
        nxt = c + 1 if d == 0 else c - 1
        prv = c - 1 if d == 0 else c + 1

        @pl.when(pos < C - 1)
        def _():
            @pl.loop(0, K)
            def _(k):
                c_copy(d, k, nxt).wait_send()

        @pl.when(pos > 0)
        def _():
            @pl.loop(0, K)
            def _(k):
                h_copy(d, k, prv).wait_send()


def body(tokens, norm_gain, expert_ids, gate_num, node_mask, w_gate, w_up, w_down):
    N = lax.axis_size("node")
    C = lax.axis_size("chip")
    T, D = tokens.shape
    SW = D // C
    FF = w_gate.shape[2]
    exp_node = EXPERTS // N
    cap = 2 * T // N
    B = N * cap
    is_first = expert_ids % exp_node == 0
    target = jnp.sum(jnp.where(is_first, expert_ids // exp_node, 0), axis=1)
    numerator = jnp.sum(jnp.where(is_first, gate_num, 0), axis=1)
    at_node = target[:, None] == jnp.arange(N, dtype=jnp.int32)[None, :]
    allowed = jnp.sum(jnp.where(at_node, node_mask, 0), axis=1)
    route_weight = (numerator * allowed).astype(F32) * (ROUTE_SCALE / DEN)
    goes = allowed == 1
    same = (target[:, None] == target[None, :]) & goes[None, :]
    earlier = jnp.arange(T)[None, :] < jnp.arange(T)[:, None]
    position = jnp.sum((same & earlier).astype(jnp.int32), axis=1)
    slot = jnp.where(goes, target * cap + position, B).astype(jnp.int32)
    slot8 = jnp.broadcast_to(slot[None, :], (8, T))
    dma = pltpu.SemaphoreType.DMA
    K = 2 * C
    GS = C // 2 + 1
    vmem = pl.BlockSpec(memory_space=pltpu.VMEM)
    hbm = pl.BlockSpec(memory_space=pl.ANY)
    return pl.pallas_call(
        functools.partial(kernel, N, C, cap),
        out_shape=jax.ShapeDtypeStruct((T, D), BF16),
        in_specs=[vmem] * 4 + [hbm] * 3,
        out_specs=vmem,
        scratch_shapes=[
            pltpu.VMEM((C, T, SW), BF16),
            pltpu.VMEM((C, T, SW), BF16),
            pltpu.VMEM((C, 8, T), jnp.int32),
            pltpu.VMEM((C, B, SW), BF16),
            pltpu.VMEM((C, B, SW), BF16),
            pltpu.VMEM((SW, 2 * FF), BF16),
            pltpu.VMEM((FF, SW), BF16),
            pltpu.VMEM((GS, B, 2 * FF), F32),
            pltpu.VMEM((2, K, B // 4, 2 * FF), BF16),
            pltpu.VMEM((C, B, FF), BF16),
            pltpu.VMEM((C, B, SW), BF16),
            pltpu.VMEM((C, B, SW), BF16),
            pltpu.VMEM((C, T, SW), BF16),
            dma((3,)),
            dma((C,)), dma((C,)), dma((C,)), dma((C,)),
            dma((C, N)), dma((C, N)),
            dma((2, K)), dma((2, K)), dma((2, K)), dma((2, K)),
            dma((C, N)), dma((C, N)),
            dma((C,)), dma((C,)),
        ],
        compiler_params=pltpu.CompilerParams(
            collective_id=0, has_side_effects=True, vmem_limit_bytes=62 * 1024 * 1024
        ),
    )(tokens, norm_gain.reshape(1, D), slot8, route_weight[:, None], w_gate, w_up, w_down)


def solution(mesh):
    placed = (
        P(("grp", "node", "chip"), None),
        P(),
        P(("grp", "node", "chip"), None),
        P(("grp", "node", "chip"), None),
        P(("grp", "node", "chip"), None),
        P("node", "chip", None),
        P("node", "chip", None),
        P("node", None, "chip"),
    )
    return jax.shard_map(
        body,
        mesh=mesh,
        in_specs=placed,
        out_specs=P(("grp", "node", "chip"), None),
        check_vma=False,
    )
```

time: 450 us -> 246 us (0.55)
  Pallas kernels: 0 us -> 240 us
  waiting for transfers between devices: 190 us -> 0 us
  blocking collectives: 173 us -> 0 us
  local copies, waits for them, and re-layouts: 42.1 us -> 4.19 us
  matrix products: 16.6 us -> 0 us
  between operations: 13.5 us -> 0.02 us
  other arithmetic: 10.2 us -> 1.62 us
    pallas_call x0 -> x1, Pallas kernels: none -> 240 us  [body(): pl.pallas_call(functools.partial(kernel, N, C, cap), out_shape=jax.ShapeD...]
    all_to_all x2 -> x0, blocking collectives: 173 us -> none  [the longest x1 86.7 us: body(): lax.all_to_all(outgoing.reshape(node_count * chip_count, capacity, slice_...]
    reduce_scatter x1 -> x0, waiting for transfers between devices: 145 us -> none  [body(): lax.psum_scatter(jnp.dot(received, w_both, preferred_element_type=jnp.flo...]
    all_gather x1 -> x0, waiting for transfers between devices: 45.2 us -> none  [body(): lax.all_gather(hidden, 'chip', axis=0, tiled=True)]
    scatter x2 -> x0, local copies, waits for them, and re-layouts: 21.4 us -> none  [body(): outgoing = outgoing.at[dest_node, :, position, :].set(pieces, mode='drop')]
    dot_general x2 -> x0, matrix products: 16.6 us -> none  [the longest x1 10 us: body(): jnp.dot(received, w_both, preferred_element_type=jnp.float32)]
    reshape x2 -> x0, local copies, waits for them, and re-layouts: 9.15 us -> none  [the longest x1 4.63 us: body(): returned = returned.reshape(node_count, chip_count, capacity, slice_width)]
    convert_element_type x4 -> x0, other arithmetic: 7 us -> none  [the longest x1 2.64 us: body(): (jax.nn.silu(own_terms[:, :hidden_units]) * own_terms[:, hidden_units:])....]
  transfers between devices with their start and end apart: 2 -> 0, of which waited for: 2 -> 0; matrix products, arithmetic and copies ran while one was open for 0% -> 0% of each run, Pallas kernels for 0% -> 0%
where the time goes in v1:
time: 246 us; the launch traced here: 245 us
  Pallas kernels  240 us (98%)
  local copies, waits for them, and re-layouts  4.19 us (2%)
    pallas_call x1, Pallas kernels, body(): pl.pallas_call(functools.partial(kernel, N, C, cap), out_shape=jax.ShapeD...  240 us

profile of v1, /device:TPU:25, one launch (start us, length us, event | category | flops | bytes accessed | tf_op | source)
XLA Modules:
  0.0 245.4 jit_solution(7365379366534868031)
XLA Ops:
  0.0 0.7 select_reduce_fusion
  0.7 0.7 select_reduce_fusion.1
  1.4 0.2 convert_reduce_fusion
  1.6 0.6 broadcast_in_dim.15.slot_in
  2.2 0.7 copy.10.weight
  3.0 239.5 %shard_map.82 = bf16[128,7168]{1,0:T(8,128)(2,1)} custom-call(bf16[128,7168]{1,0:T(8,128)(2,1)} %tok.1, f32[1,7168]{1,0:T(1,128)} %bitcast.3, s32[8,128]{1,0:T(8,128)} %broadcast_in_dim.15.slot_in, f32[128,1]{1,0:T(8,128)} %copy.10.weight, bf16[1,1792,1024]{2,1,0:T(8,128)(2,1)} %wg_hbm.1, bf16[1,1792,1024]{2,1,0:T(8,128)(2,1)} %wu_hbm.1, ...), custom_call_target="tpu_custom_call" | custom-call | tf_op jit(solution)/shard_map/pallas_call | solution.py:359
  242.5 2.8 %copy.12 = bf16[128,7168]{1,0:T(8,128)(2,1)} copy(bf16[128,7168]{1,0:T(8,128)(2,1)} %shard_map.82) | data formatting | bytes 3670016
  (3 shorter events, 0.0 us)

commit v2 on v1

--- a/solution.py
+++ b/solution.py
@@ -32,6 +32,8 @@
     K = 2 * C
     GS = partial.shape[0]
     tile = 256 if SW % 256 == 0 else 128
+    cut = (SW // tile + 1) // 2 * tile
+    parts = ((0, cut), (cut, SW - cut))
 
     def loads():
         return (
@@ -62,34 +64,58 @@
     def slot_copy(to, src):
         return remote(slot_in, slots.at[src], ss_sem.at[to], sr_sem.at[src], chip=to)
 
-    def a_copy(to, src):
-        return remote(normed.at[to], held.at[src], as_sem.at[to], ar_sem.at[src], chip=to)
-
-    def b_copy(b, to, src):
+    def a_copy(h, to, src):
+        col = pl.ds(*parts[h])
         return remote(
-            packed.at[b, pl.ds(pl.multiple_of(to * cap, cap), cap)],
-            rows.at[b, pl.ds(pl.multiple_of(src * cap, cap), cap)],
-            bs_sem.at[b, to], br_sem.at[b, src], node=to)
+            normed.at[to, :, col], held.at[src, :, col],
+            as_sem.at[h, to], ar_sem.at[h, src], chip=to)
+
+    def b_copy(h, b, to, src):
+        col = pl.ds(*parts[h])
+        return remote(
+            packed.at[b, pl.ds(pl.multiple_of(to * cap, cap), cap), col],
+            rows.at[b, pl.ds(pl.multiple_of(src * cap, cap), cap), col],
+            bs_sem.at[h, b, to], br_sem.at[h, b, src], node=to)
 
     def c_copy(d, k, to):
         return remote(sums.at[d, k], sums.at[d, k], cs_sem.at[d, k], cr_sem.at[d, k], chip=to)
 
+    def order(d, i):
+        p = lax.div(i, 2)
+        return jnp.where(lax.rem(i, 2) == d, p, C - 1 - p)
+
     def place(d, k):
-        return lax.div(k, 2), pl.multiple_of(d * 2 * R + lax.rem(k, 2) * R, R)
+        return order(d, lax.div(k, 2)), pl.multiple_of(d * 2 * R + lax.rem(k, 2) * R, R)
+
+    low = jnp.where(c < C // 2, 0, 1)
+
+    def kept(d, k):
+        i = lax.div(k, 2)
+        return lax.rem(jnp.where(low == d, i, i + 1 - 2 * lax.rem(i, 2)), GS)
 
     def h_copy(d, k, to):
         b, r = place(d, k)
         piece = hidden.at[b, pl.ds(r, R)]
         return remote(piece, piece, hs_sem.at[d, k], hr_sem.at[d, k], chip=to)
 
-    def d_copy(b, to, src):
+    def d_copy(h, b, to, src):
+        col = pl.ds(*parts[h])
         return remote(
-            made.at[b, pl.ds(pl.multiple_of(to * cap, cap), cap)],
-            back.at[b, pl.ds(pl.multiple_of(src * cap, cap), cap)],
-            ds_sem.at[b, to], dr_sem.at[b, src], node=to)
-
-    def e_copy(to, src):
-        return remote(held.at[to], final.at[src], es_sem.at[to], er_sem.at[src], chip=to)
+            made.at[b, pl.ds(pl.multiple_of(to * cap, cap), cap), col],
+            back.at[b, pl.ds(pl.multiple_of(src * cap, cap), cap), col],
+            ds_sem.at[h, b, to], dr_sem.at[h, b, src], node=to)
+
+    def e_copy(h, to, src):
+        col = pl.ds(*parts[h])
+        return remote(
+            held.at[to, :, col], final.at[src, :, col],
+            es_sem.at[h, to], er_sem.at[h, src], chip=to)
+
+    def tiles(h):
+        return parts[h][1] // tile
+
+    def at(h, i):
+        return pl.multiple_of(parts[h][0] + i * tile, tile)
 
     def squares(i, acc):
         v = tok[:, pl.ds(pl.multiple_of(i * tile, tile), tile)].astype(F32)
@@ -100,50 +126,63 @@
 
     pl.semaphore_wait(barrier, C + N - 2)
 
-    def normalise(to):
-        @pl.loop(0, SW // tile)
+    def normalise(h, to):
+        @pl.loop(0, tiles(h))
         def _(i):
-            col = pl.multiple_of(to * SW + i * tile, tile)
+            col = pl.multiple_of(to * SW + at(h, i), tile)
             v = tok[:, pl.ds(col, tile)].astype(F32)
             v = v * inverse * gain[:, pl.ds(col, tile)]
-            normed[to, :, pl.ds(pl.multiple_of(i * tile, tile), tile)] = v.astype(BF16)
+            normed[to, :, pl.ds(at(h, i), tile)] = v.astype(BF16)
 
     @pl.loop(1, C)
     def _(r):
         to = lax.rem(c + r, C)
         slot_copy(to, c).start()
-        normalise(to)
-        a_copy(to, c).start()
-
-    normalise(c)
-
-    def route(source, b, rows_of_slots):
-        @pl.loop(0, SW // tile)
+        normalise(0, to)
+        a_copy(0, to, c).start()
+
+    @pl.loop(1, C)
+    def _(r):
+        to = lax.rem(c + r, C)
+        normalise(1, to)
+        a_copy(1, to, c).start()
+
+    def route(h, source, b, rows_of_slots):
+        @pl.loop(0, tiles(h))
         def _(i):
-            col = pl.ds(pl.multiple_of(i * tile, tile), tile)
+            col = pl.ds(at(h, i), tile)
             packed[b, :, col] = jnp.dot(
                 rows_of_slots, source[b, :, col], preferred_element_type=F32).astype(BF16)
 
         @pl.loop(1, N)
         def _(r):
-            b_copy(b, lax.rem(n + r, N), n).start()
+            b_copy(h, b, lax.rem(n + r, N), n).start()
 
         own = pl.ds(pl.multiple_of(n * cap, cap), cap)
-        rows[b, own, :] = packed[b, own, :]
+        part = pl.ds(*parts[h])
+        rows[b, own, part] = packed[b, own, part]
 
     def selector(slot_row):
         ids = lax.broadcasted_iota(jnp.int32, (B, T), 0)
         return jnp.where(ids == slot_row, 1.0, 0.0).astype(BF16)
 
     slots[c] = slot_in[...]
-    route(normed, c, selector(slot_in[0:1, :]))
+    for h in (0, 1):
+        normalise(h, c)
+        route(h, normed, c, selector(slot_in[0:1, :]))
 
     @pl.loop(1, C)
     def _(r):
         b = lax.rem(c + r, C)
         slot_copy(b, b).wait_recv()
-        a_copy(b, b).wait_recv()
-        route(held, b, selector(slots[b, 0:1, :]))
+        a_copy(0, b, b).wait_recv()
+        route(0, held, b, selector(slots[b, 0:1, :]))
+
+    @pl.loop(1, C)
+    def _(r):
+        b = lax.rem(c + r, C)
+        a_copy(1, b, b).wait_recv()
+        route(1, held, b, selector(slots[b, 0:1, :]))
 
     copies = loads()
     copies[0].wait()
@@ -156,19 +195,22 @@
 
     @pl.loop(0, K + 2 * (C - 1) + 2)
     def _(t):
-        blk = lax.div(t, 2)
-
-        @pl.when((lax.rem(t, 2) == 0) & (blk < C))
+        turn = lax.div(t, 2)
+
+        @pl.when((lax.rem(t, 2) == 0) & (turn < C))
         def _():
+            blk = order(low, turn)
+
             @pl.loop(1, N)
             def _(r):
                 src = lax.rem(n + r, N)
-                b_copy(blk, src, src).wait_recv()
+                b_copy(0, blk, src, src).wait_recv()
+                b_copy(1, blk, src, src).wait_recv()
 
             @pl.loop(0, 2 * FF // wide)
             def _(i):
                 col = pl.ds(pl.multiple_of(i * wide, wide), wide)
-                partial[lax.rem(blk, GS), :, col] = jnp.dot(
+                partial[lax.rem(turn, GS), :, col] = jnp.dot(
                     rows[blk], wgu[:, col], preferred_element_type=F32)
 
         for d in (0, 1):
@@ -185,7 +227,7 @@
                 def _(i):
                     o = pl.multiple_of(i * thin, thin)
                     sums[d, k, pl.ds(o, thin), :] = partial[
-                        lax.rem(b, GS), pl.ds(r + o, thin), :].astype(BF16)
+                        kept(d, k), pl.ds(r + o, thin), :].astype(BF16)
 
                 c_copy(d, k, nxt).start()
 
@@ -198,7 +240,7 @@
                 def _(i):
                     o = pl.multiple_of(i * thin, thin)
                     s = sums[d, k, pl.ds(o, thin), :].astype(F32)
-                    s += partial[lax.rem(b, GS), pl.ds(r + o, thin), :]
+                    s += partial[kept(d, k), pl.ds(r + o, thin), :]
                     sums[d, k, pl.ds(o, thin), :] = s.astype(BF16)
 
                 c_copy(d, k, nxt).start()
@@ -212,7 +254,7 @@
                 def _(i):
                     o = pl.multiple_of(i * thin, thin)
                     s = sums[d, k, pl.ds(o, thin), :].astype(F32)
-                    s += partial[lax.rem(b, GS), pl.ds(r + o, thin), :]
+                    s += partial[kept(d, k), pl.ds(r + o, thin), :]
                     g, u = s[:, :FF], s[:, FF:]
                     hidden[b, pl.ds(r + o, thin), :] = (
                         g * (1.0 / (1.0 + jnp.exp(-g))) * u).astype(BF16)
@@ -235,82 +277,94 @@
 
         e = t - ahead
 
-        @pl.when((e >= 0) & (lax.rem(e, 2) == 1) & (e < K))
+        @pl.when((e >= 0) & (lax.rem(e, 4) == 3) & (e < K))
         def _():
-            b = lax.div(e, 2)
-
-            @pl.loop(0, SW // tile)
-            def _(i):
-                col = pl.ds(pl.multiple_of(i * tile, tile), tile)
-                made[b, :, col] = jnp.dot(
-                    hidden[b], wd[:, col], preferred_element_type=F32).astype(BF16)
-
-            @pl.loop(1, N)
-            def _(r):
-                d_copy(b, lax.rem(n + r, N), n).start()
-
-            own = pl.ds(pl.multiple_of(n * cap, cap), cap)
-            back[b, own, :] = made[b, own, :]
+            pair = lax.div(e, 4)
+            for h in (0, 1):
+                @pl.loop(0, 2)
+                def _(m):
+                    b = order(0, 2 * pair + m)
+
+                    @pl.loop(0, tiles(h))
+                    def _(i):
+                        col = pl.ds(at(h, i), tile)
+                        made[b, :, col] = jnp.dot(
+                            hidden[b], wd[:, col], preferred_element_type=F32).astype(BF16)
+
+                    @pl.loop(1, N)
+                    def _(r):
+                        d_copy(h, b, lax.rem(n + r, N), n).start()
+
+                    own = pl.ds(pl.multiple_of(n * cap, cap), cap)
+                    part = pl.ds(*parts[h])
+                    back[b, own, part] = made[b, own, part]
 
         f = t - ahead - 2
 
-        @pl.when((f >= 0) & (lax.rem(f, 2) == 1) & (f < K))
+        @pl.when((f >= 0) & (lax.rem(f, 4) == 3) & (f < K))
         def _():
-            b = lax.div(f, 2)
-
-            @pl.loop(1, N)
-            def _(r):
-                src = lax.rem(n + r, N)
-                d_copy(b, src, src).wait_recv()
-
-            pick = selector(slots[b, 0:1, :])
-
-            def give(place_to):
-                @pl.loop(0, SW // tile)
-                def _(i):
-                    col = pl.ds(pl.multiple_of(i * tile, tile), tile)
-                    place_to[b, :, col] = lax.dot_general(
-                        pick, back[b, :, col], (((0,), (0,)), ((), ())),
-                        preferred_element_type=F32).astype(BF16)
-
-            @pl.when(b == c)
-            def _():
-                give(final)
-
-            @pl.when(b != c)
-            def _():
-                give(held)
-                e_copy(b, c).start()
-
-    def finish(src):
-        @pl.loop(0, SW // tile)
+            pair = lax.div(f, 4)
+            for h in (0, 1):
+                @pl.loop(0, 2)
+                def _(m):
+                    b = order(0, 2 * pair + m)
+
+                    @pl.loop(1, N)
+                    def _(r):
+                        src = lax.rem(n + r, N)
+                        d_copy(h, b, src, src).wait_recv()
+
+                    pick = selector(slots[b, 0:1, :])
+
+                    def give(place_to):
+                        @pl.loop(0, tiles(h))
+                        def _(i):
+                            col = pl.ds(at(h, i), tile)
+                            place_to[b, :, col] = lax.dot_general(
+                                pick, back[b, :, col], (((0,), (0,)), ((), ())),
+                                preferred_element_type=F32).astype(BF16)
+
+                    @pl.when(b == c)
+                    def _():
+                        give(final)
+
+                    @pl.when(b != c)
+                    def _():
+                        give(held)
+                        e_copy(h, b, c).start()
+
+    def finish(h, src):
+        @pl.loop(0, tiles(h))
         def _(i):
-            col = pl.ds(pl.multiple_of(src * SW + i * tile, tile), tile)
-            v = final[src, :, pl.ds(pl.multiple_of(i * tile, tile), tile)].astype(F32)
+            col = pl.ds(pl.multiple_of(src * SW + at(h, i), tile), tile)
+            v = final[src, :, pl.ds(at(h, i), tile)].astype(F32)
             out[:, col] = (tok[:, col].astype(F32) + weight[...] * v).astype(BF16)
 
-    finish(c)
-
-    @pl.loop(1, C)
-    def _(r):
-        src = lax.rem(c + r, C)
-        e_copy(src, src).wait_recv()
-        finish(src)
+    for h in (0, 1):
+        finish(h, c)
+
+        @pl.loop(1, C)
+        def _(r):
+            src = lax.rem(c + r, C)
+            e_copy(h, src, src).wait_recv()
+            finish(h, src)
 
     @pl.loop(1, C)
     def _(r):
         to = lax.rem(c + r, C)
         slot_copy(to, c).wait_send()
-        a_copy(to, c).wait_send()
-        e_copy(to, c).wait_send()
+        for h in (0, 1):
+            a_copy(h, to, c).wait_send()
+            e_copy(h, to, c).wait_send()
 
     @pl.loop(0, C)
     def _(b):
         @pl.loop(1, N)
         def _(r):
             to = lax.rem(n + r, N)
-            b_copy(b, to, n).wait_send()
-            d_copy(b, to, n).wait_send()
+            for h in (0, 1):
+                b_copy(h, b, to, n).wait_send()
+                d_copy(h, b, to, n).wait_send()
 
     for d in (0, 1):
         pos = c if d == 0 else C - 1 - c
@@ -353,7 +407,7 @@
     slot8 = jnp.broadcast_to(slot[None, :], (8, T))
     dma = pltpu.SemaphoreType.DMA
     K = 2 * C
-    GS = C // 2 + 1
+    GS = C // 2 + 2
     vmem = pl.BlockSpec(memory_space=pltpu.VMEM)
     hbm = pl.BlockSpec(memory_space=pl.ANY)
     return pl.pallas_call(
@@ -376,11 +430,11 @@
             pltpu.VMEM((C, B, SW), BF16),
             pltpu.VMEM((C, T, SW), BF16),
             dma((3,)),
-            dma((C,)), dma((C,)), dma((C,)), dma((C,)),
-            dma((C, N)), dma((C, N)),
+            dma((C,)), dma((C,)), dma((2, C)), dma((2, C)),
+            dma((2, C, N)), dma((2, C, N)),
             dma((2, K)), dma((2, K)), dma((2, K)), dma((2, K)),
-            dma((C, N)), dma((C, N)),
-            dma((C,)), dma((C,)),
+            dma((2, C, N)), dma((2, C, N)),
+            dma((2, C)), dma((2, C)),
         ],
         compiler_params=pltpu.CompilerParams(
             collective_id=0, has_side_effects=True, vmem_limit_bytes=62 * 1024 * 1024

time: 246 us -> 225 us (0.915)
  Pallas kernels: 240 us -> 216 us
    pallas_call x1, Pallas kernels: 240 us -> 216 us  [body(): pl.pallas_call(functools.partial(kernel, N, C, cap), out_shape=jax.ShapeD...]
where the time goes in v2:
time: 225 us; the launch traced here: 222 us
  Pallas kernels  216 us (96%)
  local copies, waits for them, and re-layouts  4.19 us (2%)
    pallas_call x1, Pallas kernels, body(): pl.pallas_call(functools.partial(kernel, N, C, cap), out_shape=jax.ShapeD...  216 us

profile of v2, /device:TPU:25, one launch (start us, length us, event | category | flops | bytes accessed | tf_op | source)
XLA Modules:
  0.0 222.3 jit_solution(8236209617277753992)
XLA Ops:
  0.0 0.7 select_reduce_fusion
  0.7 0.7 select_reduce_fusion.1
  1.4 0.2 convert_reduce_fusion
  1.6 0.6 broadcast_in_dim.15.slot_in
  2.2 0.7 copy.10.weight
  3.0 216.5 %shard_map.82 = bf16[128,7168]{1,0:T(8,128)(2,1)} custom-call(bf16[128,7168]{1,0:T(8,128)(2,1)} %tok.1, f32[1,7168]{1,0:T(1,128)} %bitcast.3, s32[8,128]{1,0:T(8,128)} %broadcast_in_dim.15.slot_in, f32[128,1]{1,0:T(8,128)} %copy.10.weight, bf16[1,1792,1024]{2,1,0:T(8,128)(2,1)} %wg_hbm.1, bf16[1,1792,1024]{2,1,0:T(8,128)(2,1)} %wu_hbm.1, ...), custom_call_target="tpu_custom_call" | custom-call | tf_op jit(solution)/shard_map/pallas_call | solution.py:413
  219.5 2.8 %copy.12 = bf16[128,7168]{1,0:T(8,128)(2,1)} copy(bf16[128,7168]{1,0:T(8,128)(2,1)} %shard_map.82) | data formatting | bytes 3670016
  (3 shorter events, 0.0 us)

commit v3 on v2

--- a/solution.py
+++ b/solution.py
@@ -12,6 +12,7 @@
 ROUTE_SCALE = 2.827
 F32 = jnp.float32
 BF16 = jnp.bfloat16
+PARTS = 4
 
 
 def kernel(
@@ -32,8 +33,9 @@
     K = 2 * C
     GS = partial.shape[0]
     tile = 256 if SW % 256 == 0 else 128
-    cut = (SW // tile + 1) // 2 * tile
-    parts = ((0, cut), (cut, SW - cut))
+    step = -(-SW // tile // PARTS) * tile
+    parts = [(o, min(step, SW - o)) for o in range(0, SW, step)]
+    every = range(len(parts))
 
     def loads():
         return (
@@ -141,11 +143,12 @@
         normalise(0, to)
         a_copy(0, to, c).start()
 
-    @pl.loop(1, C)
-    def _(r):
-        to = lax.rem(c + r, C)
-        normalise(1, to)
-        a_copy(1, to, c).start()
+    for h in every[1:]:
+        @pl.loop(1, C)
+        def _(r):
+            to = lax.rem(c + r, C)
+            normalise(h, to)
+            a_copy(h, to, c).start()
 
     def route(h, source, b, rows_of_slots):
         @pl.loop(0, tiles(h))
@@ -167,22 +170,20 @@
         return jnp.where(ids == slot_row, 1.0, 0.0).astype(BF16)
 
     slots[c] = slot_in[...]
-    for h in (0, 1):
+    for h in every:
         normalise(h, c)
         route(h, normed, c, selector(slot_in[0:1, :]))
 
-    @pl.loop(1, C)
-    def _(r):
-        b = lax.rem(c + r, C)
-        slot_copy(b, b).wait_recv()
-        a_copy(0, b, b).wait_recv()
-        route(0, held, b, selector(slots[b, 0:1, :]))
-
-    @pl.loop(1, C)
-    def _(r):
-        b = lax.rem(c + r, C)
-        a_copy(1, b, b).wait_recv()
-        route(1, held, b, selector(slots[b, 0:1, :]))
+    def bring(b):
+        @pl.when(b != c)
+        def _():
+            slot_copy(b, b).wait_recv()
+            pick = selector(slots[b, 0:1, :])
+            for h in every:
+                a_copy(h, b, b).wait_recv()
+                route(h, held, b, pick)
+
+    bring(order(low, 0))
 
     copies = loads()
     copies[0].wait()
@@ -204,8 +205,8 @@
             @pl.loop(1, N)
             def _(r):
                 src = lax.rem(n + r, N)
-                b_copy(0, blk, src, src).wait_recv()
-                b_copy(1, blk, src, src).wait_recv()
+                for h in every:
+                    b_copy(h, blk, src, src).wait_recv()
 
             @pl.loop(0, 2 * FF // wide)
             def _(i):
@@ -275,12 +276,16 @@
                 def _():
                     h_copy(d, k, prv).start()
 
+        @pl.when((lax.rem(t, 2) == 0) & (turn < C - 1))
+        def _():
+            bring(order(low, turn + 1))
+
         e = t - ahead
 
         @pl.when((e >= 0) & (lax.rem(e, 4) == 3) & (e < K))
         def _():
             pair = lax.div(e, 4)
-            for h in (0, 1):
+            for h in every:
                 @pl.loop(0, 2)
                 def _(m):
                     b = order(0, 2 * pair + m)
@@ -304,7 +309,7 @@
         @pl.when((f >= 0) & (lax.rem(f, 4) == 3) & (f < K))
         def _():
             pair = lax.div(f, 4)
-            for h in (0, 1):
+            for h in every:
                 @pl.loop(0, 2)
                 def _(m):
                     b = order(0, 2 * pair + m)
@@ -340,7 +345,7 @@
             v = final[src, :, pl.ds(at(h, i), tile)].astype(F32)
             out[:, col] = (tok[:, col].astype(F32) + weight[...] * v).astype(BF16)
 
-    for h in (0, 1):
+    for h in every:
         finish(h, c)
 
         @pl.loop(1, C)
@@ -353,7 +358,7 @@
     def _(r):
         to = lax.rem(c + r, C)
         slot_copy(to, c).wait_send()
-        for h in (0, 1):
+        for h in every:
             a_copy(h, to, c).wait_send()
             e_copy(h, to, c).wait_send()
 
@@ -362,7 +367,7 @@
         @pl.loop(1, N)
         def _(r):
             to = lax.rem(n + r, N)
-            for h in (0, 1):
+            for h in every:
                 b_copy(h, b, to, n).wait_send()
                 d_copy(h, b, to, n).wait_send()
 
@@ -430,11 +435,11 @@
             pltpu.VMEM((C, B, SW), BF16),
             pltpu.VMEM((C, T, SW), BF16),
             dma((3,)),
-            dma((C,)), dma((C,)), dma((2, C)), dma((2, C)),
-            dma((2, C, N)), dma((2, C, N)),
+            dma((C,)), dma((C,)), dma((PARTS, C)), dma((PARTS, C)),
+            dma((PARTS, C, N)), dma((PARTS, C, N)),
             dma((2, K)), dma((2, K)), dma((2, K)), dma((2, K)),
-            dma((2, C, N)), dma((2, C, N)),
-            dma((2, C)), dma((2, C)),
+            dma((PARTS, C, N)), dma((PARTS, C, N)),
+            dma((PARTS, C)), dma((PARTS, C)),
         ],
         compiler_params=pltpu.CompilerParams(
             collective_id=0, has_side_effects=True, vmem_limit_bytes=62 * 1024 * 1024

time: 225 us -> 202 us (0.90)
  Pallas kernels: 216 us -> 193 us
    pallas_call x1, Pallas kernels: 216 us -> 193 us  [body(): pl.pallas_call(functools.partial(kernel, N, C, cap), out_shape=jax.ShapeD...]
where the time goes in v3:
time: 202 us; the launch traced here: 199 us
  Pallas kernels  193 us (96%)
  local copies, waits for them, and re-layouts  4.19 us (2%)
    pallas_call x1, Pallas kernels, body(): pl.pallas_call(functools.partial(kernel, N, C, cap), out_shape=jax.ShapeD...  193 us

profile of v3, /device:TPU:25, one launch (start us, length us, event | category | flops | bytes accessed | tf_op | source)
XLA Modules:
  0.0 199.2 jit_solution(14628777934744646257)
XLA Ops:
  0.0 0.7 select_reduce_fusion
  0.7 0.7 select_reduce_fusion.1
  1.4 0.2 convert_reduce_fusion
  1.6 0.6 broadcast_in_dim.15.slot_in
  2.2 0.7 copy.10.weight
  3.0 193.3 %shard_map.82 = bf16[128,7168]{1,0:T(8,128)(2,1)} custom-call(bf16[128,7168]{1,0:T(8,128)(2,1)} %tok.1, f32[1,7168]{1,0:T(1,128)} %bitcast.3, s32[8,128]{1,0:T(8,128)} %broadcast_in_dim.15.slot_in, f32[128,1]{1,0:T(8,128)} %copy.10.weight, bf16[1,1792,1024]{2,1,0:T(8,128)(2,1)} %wg_hbm.1, bf16[1,1792,1024]{2,1,0:T(8,128)(2,1)} %wu_hbm.1, ...), custom_call_target="tpu_custom_call" | custom-call | tf_op jit(solution)/shard_map/pallas_call | solution.py:418
  196.3 2.8 %copy.12 = bf16[128,7168]{1,0:T(8,128)(2,1)} copy(bf16[128,7168]{1,0:T(8,128)(2,1)} %shard_map.82) | data formatting | bytes 3670016
  (3 shorter events, 0.0 us)
